TPU v7x, 128 devices: a whole 4x4x4 slice. The times are simulated.
128 devices in a mesh: doc: 4 (over z_lo, core), param: 32 (over x, z_hi, y).
Axes of the slice: x: 4, y: 4, z: 4 (z_hi: 2, z_lo: 2; z = z_hi * 2 + z_lo), core: 2. Of those that a mesh axis runs over, the one named last changes fastest.
Arguments:
- layer_input: bfloat16 [2048, 8192], P('doc', 'param'), may hold values from -6 to 6
- output_grad: bfloat16 [2048, 8192], P('doc', 'param'), may hold values from -0.29882812 to 0.29882812
- doc_ids: int32 [2048], P('doc'), may hold values from 0 to 3, never falling along the last dimension, each value on 1 to 1536 neighbouring positions
- sign_bits: int32 [8192, 8192], P('param'), may hold values from 0 to 1
- kept_rows: int32 [8192], replicated, may hold values from 0 to 8191
- kept_cols: int32 [8192], replicated, may hold values from 0 to 8191
Outputs:
- sketch: float32 [4, 8192], P('doc', 'param')
Inputs may be any that keep to these rules, and one draw needn't show every extreme that they name: `doc_ids`: document numbers never fall along the packed rows; every document has 1 to 1536 rows and one has exactly 1536.
All inputs are finite; a program needn't handle non-finite values.
Results may differ from a plain program's by a relative error of at most 0.0003.
Values may be sent and summed in bfloat16 or wider, within the bound.
A program may use at most 128 MiB of HBM per device.

v0:
```python
import jax
import jax.numpy as jnp
from jax import lax
from jax.sharding import PartitionSpec as P

MOST = 1536


def sign_table(size):
    index = jnp.arange(size, dtype=jnp.int32)
    common = index[:, None] & index[None, :]
    count = jnp.zeros((size, size), jnp.int32)
    for bit in range(max(size.bit_length() - 1, 1)):
        count = count + (common >> bit & 1)
    return (1 - 2 * (count % 2)).astype(jnp.float32)


def hadamard(block3, length):
    lead, middle, tail = block3.shape
    done = 1
    while done < length:
        factor = min(128, length // done)
        view = block3.reshape(lead * done, factor, length // (done * factor) * tail)
        view = jnp.einsum("afb,gf->agb", view, sign_table(factor), precision=lax.Precision.HIGHEST)
        block3 = view.reshape(lead, length, tail)
        done = done * factor
    return block3


def on_device(layer_input, output_grad, doc_ids, sign_bits, kept_rows, kept_cols):
    owner = lax.axis_index("doc")
    rank = lax.axis_index("param")
    parts = lax.axis_size("param")
    block = layer_input.shape[1]
    width = sign_bits.shape[1]
    stacked = jnp.concatenate([layer_input, output_grad], axis=1)
    every_id = lax.all_gather(doc_ids, "doc", axis=0, tiled=True)
    all_stacked = lax.all_gather(stacked, "doc", axis=0, tiled=True)
    first = jnp.sum((every_id < owner).astype(jnp.int32))
    length = jnp.sum((every_id == owner).astype(jnp.int32))
    extended = jnp.concatenate([all_stacked, jnp.zeros((MOST, 2 * block), jnp.bfloat16)], axis=0)
    window = lax.dynamic_slice_in_dim(extended, first, MOST, 0)
    within = (jnp.arange(MOST, dtype=jnp.int32) < length)[:, None]
    gathered_rows = jnp.where(within, window, 0)
    inputs_part = gathered_rows[:, :block]
    grads_part = gathered_rows[:, block:]
    gradient = lax.dot_general(
        inputs_part,
        lax.all_gather(grads_part, "param", axis=1, tiled=True),
        (((0,), (0,)), ((), ())),
        preferred_element_type=jnp.float32,
    )
    signed = gradient * (2 * sign_bits - 1).astype(jnp.float32)
    mixed = hadamard(signed.reshape(1, block, width), block)
    mixed = hadamard(mixed.reshape(block, width, 1), width).reshape(block, width)
    slab = width // parts
    moved = lax.all_to_all(mixed, "param", split_axis=1, concat_axis=0, tiled=True)
    whole = hadamard(moved.reshape(1, parts, block * slab), parts).reshape(parts * block, slab)
    local_col = kept_cols - rank * slab
    mine = kept_cols // slab == rank
    flat = kept_rows * slab + jnp.clip(local_col, 0, slab - 1)
    value = whole.reshape(-1)[flat]
    term = jnp.where(mine, value, 0.0) / width
    share = lax.psum_scatter(term, "param", scatter_dimension=0, tiled=True)
    return share.reshape(1, -1)


def solution(mesh):
    placed = (P("doc", "param"), P("doc", "param"), P("doc"), P("param", None), P(), P())
    return jax.shard_map(
        on_device, mesh=mesh, in_specs=placed, out_specs=P("doc", "param"), check_vma=False
    )
```

profile of v0, /device:TPU:0, one launch (start us, length us, event | category | flops | bytes accessed | tf_op | source)
XLA Modules:
  0.0 982.8 jit_solution(12321764363066140593)
XLA Ops:
  6.5 0.0 all-gather.4.cloned.1.call-start
  6.5 1.9 pad_maximum_fusion
  8.4 0.0 all-gather.4.cloned.1.call-update
  8.4 0.0 all-gather.6.cloned.1.call-start
  8.5 5.3 all-gather
  13.8 0.7 fusion.53
  16.6 0.7 iota_compare_fusion
  17.3 23.2 %all-gather.4.cloned.1.call-done = bf16[2048,512]{1,0:T(8,128)(2,1)} async-done(((bf16[512,512]{1,0:T(8,128)(2,1)}), bf16[2048,512]{1,0:T(8,128)(2,1)}) %all-gather.4.cloned.1.call-update) | async-done | bytes 2097168 | tf_op jit(solution)/shard_map/all_gather | solution.py:38
  40.5 2.1 fusion.3
  42.6 1.0 slice.11
  43.6 0.0 all-gather.6.cloned.1.call-update
  43.6 288.0 %all-gather.6.cloned.1.call-done = bf16[1536,8192]{1,0:T(8,128)(2,1)} async-done(((bf16[1536,256]{1,0:T(8,128)(2,1)}), bf16[1536,8192]{1,0:T(8,128)(2,1)}) %all-gather.6.cloned.1.call-update) | async-done | bytes 25165840 | tf_op jit(solution)/shard_map/all_gather | solution.py:49
  331.5 19.9 %convolution_multiply_fusion = f32[256,8192]{1,0:T(8,128)} fusion(bf16[1536,8192]{1,0:T(8,128)(2,1)} %all-gather.6.cloned.1.call-done, s32[256,8192]{1,0:T(8,128)} %param.9, bf16[1536,512]{1,0:T(8,128)(2,1)S(1)} %fusion.3), kind=kOutput, calls=%fused_computation.2 | convolution fusion | flops 6450839552 | bytes 42729472 | tf_op jit(solution)/shard_map/dot_general | solution.py:47
  351.4 9.9 %reshape.31 = f32[128,16384]{1,0:T(8,128)} reshape(f32[256,8192]{1,0:T(8,128)} %convolution_multiply_fusion) | data formatting | bytes 16777216 | tf_op jit(solution)/shard_map/reshape
  361.4 9.0 copy.12
  370.3 10.1 %fusion.11 = f32[128,2,8192]{2,0,1:T(8,128)S(1)} fusion(f32[2,8192,128]{2,1,0:T(8,128)} %bitcast.40), kind=kOutput, calls=%fused_computation.22 | convolution fusion | flops 3221798912 | bytes 16777216 | tf_op jit(solution)/shard_map/afb,gf->agb/dot_general | solution.py:24
  380.4 34.5 %convolution_bitcast_fusion.1 = f32[128,2,8192]{2,1,0:T(2,128)} fusion(f32[128,2,8192]{2,0,1:T(8,128)S(1)} %fusion.11), kind=kOutput, calls=%fused_computation.3 | convolution fusion | flops 50331716 | bytes 16777216 | tf_op jit(solution)/shard_map/afb,gf->agb/dot_general | solution.py:24
  414.8 16.5 %reshape_reshape_reshape.3 = f32[256,128,64]{2,1,0:T(8,128)} reshape(f32[128,2,8192]{2,1,0:T(2,128)} %convolution_bitcast_fusion.1) | data formatting | bytes 16777216 | tf_op jit(solution)/shard_map/reshape;reshape;reshape | solution.py:23
  431.3 14.0 %copy.14 = f32[256,128,64]{1,0,2:T(8,128)} copy(f32[256,128,64]{2,1,0:T(8,128)} %reshape_reshape_reshape.3) | data formatting | bytes 16777216 | tf_op jit(solution)/shard_map/reshape;reshape;reshape | solution.py:23
  445.3 14.0 %convolution_bitcast_fusion.3 = f32[256,128,64]{0,1,2:T(8,128)} fusion(f32[256,128,64]{1,0,2:T(8,128)} %copy.14), kind=kOutput, calls=%fused_computation.9 | convolution fusion | flops 3221798912 | bytes 16777216 | tf_op jit(solution)/shard_map/afb,gf->agb/dot_general | solution.py:24
  459.3 9.0 copy.15
  468.3 17.5 %convolution_bitcast_fusion = f32[32768,64,1]{0,1,2:T(8,128)} fusion(f32[8,8,256,128]{3,2,1,0:T(8,128)} %bitcast.41), kind=kOutput, calls=%fused_computation.1 | convolution fusion | flops 1610743808 | bytes 16777216 | tf_op jit(solution)/shard_map/afb,gf->agb/dot_general | solution.py:24
  485.8 12.2 %copy.16 = f32[32768,64,1]{1,0,2:T(8,128)} copy(f32[32768,64,1]{0,1,2:T(8,128)} %convolution_bitcast_fusion) | data formatting | bytes 16777216 | tf_op jit(solution)/shard_map/afb,gf->agb/transpose | solution.py:24
  498.0 14.4 %all_to_all.12 = f32[256,32,256]{2,1,0:T(8,128)} reshape(f32[32768,64,1]{1,0,2:T(8,128)} %copy.16) | data formatting | bytes 16777216 | tf_op jit(solution)/shard_map/all_to_all | solution.py:57
  512.4 11.5 %copy.17 = f32[256,32,256]{2,0,1:T(8,128)} copy(f32[256,32,256]{2,1,0:T(8,128)} %all_to_all.12) | data formatting | bytes 16777216 | tf_op jit(solution)/shard_map/all_to_all | solution.py:57
  523.8 0.0 copy-start.2
  523.8 0.0 copy-start
  523.8 0.0 copy-start.1
  523.8 5.3 all-to-all-start
  529.2 0.0 copy-done.2
  529.2 0.6 dynamic-slice
  530.4 0.0 copy-done
  530.5 0.0 copy-done.1
  530.5 147.1 %all-to-all-done = f32[256,32,256]{2,0,1:T(8,128)} async-done(((f32[256,32,256]{2,0,1:T(8,128)}), f32[256,32,256]{2,0,1:T(8,128)}, u32[]{:S(2)}, u32[]{:S(2)}) %all-to-all-start) | async-done | bytes 8388640 | tf_op jit(solution)/shard_map/all_to_all | solution.py:57
  677.6 8.2 copy.19
  685.8 8.4 convolution_bitcast_fusion.2
  694.2 4.7 copy.20
  698.9 96.4 %gather_fusion = f32[8192]{0:T(1024)S(1)} fusion(f32[2097152]{0:T(1024)} %bitcast.38, s32[8192]{0:T(1024)S(1)} %fusion.20), kind=kCustom, calls=%fused_computation | custom fusion | bytes 98304 | tf_op jit(solution)/shard_map/gather | solution.py:62
  795.3 179.6 %all-reduce.1 = f32[8192]{0:T(1024)S(1)} all-reduce(f32[8192]{0:T(1024)S(1)} %select_multiply_fusion), channel_id=2, replica_groups=mesh['doc'=4,'param'=32] {'param'}, use_global_device_ids=true, to_apply=%region_2.3.clone | all-reduce | flops 8192 | bytes 65536
  974.9 0.6 dynamic-slice.1
  (2 shorter events, 0.1 us)
Async XLA Ops:
  6.5 34.0 %all-gather.4.cloned.1.call-start = ((), (), s32[]{:S(2)}) async-start(), calls=%async_computation.1 | async-start | bytes 2621440 | tf_op jit(solution)/shard_map/all_gather | solution.py:38
  8.4 323.1 %all-gather.6.cloned.1.call-start = ((), (), s32[]{:S(2)}) async-start(), calls=%async_computation.2 | async-start | bytes 25952256 | tf_op jit(solution)/shard_map/all_gather | solution.py:49
  523.8 5.4 copy-start.2
  523.8 6.6 copy-start
  523.8 6.6 copy-start.1
  523.8 153.7 %all-to-all-start = ((f32[256,32,256]{2,0,1:T(8,128)}), f32[256,32,256]{2,0,1:T(8,128)}, u32[]{:S(2)}, u32[]{:S(2)}) async-start(f32[256,32,256]{2,0,1:T(8,128)} %copy.17), calls=%async_computation | async-start | bytes 16777216 | tf_op jit(solution)/shard_map/all_to_all | solution.py:57
Sparse Core Ops, SparseCore 0:
  9.0 31.4 all-gather.3
  43.7 287.7 all-gather.5
where the time goes:
time: 995 us; the launch traced here: 983 us
  waiting for transfers between devices  458 us (46%)
  local copies, waits for them, and re-layouts  208 us (21%)
  blocking collectives  185 us (19%)
  matrix products  104 us (10%)
  between operations  16.7 us (2%)
    all_gather x1, waiting for transfers between devices, on_device(): lax.all_gather(grads_part, 'param', axis=1, tiled=True)  288 us
    unnamed x1, blocking collectives  180 us
    all_to_all x1, waiting for transfers between devices, on_device(): lax.all_to_all(mixed, 'param', split_axis=1, concat_axis=0, tiled=True)  147 us
    gather x1, local copies, waits for them, and re-layouts, on_device(): value = whole.reshape(-1)[flat]  96.4 us
    dot_general x5, matrix products, hadamard(): jnp.einsum('afb,gf->agb', view, sign_table(factor), precision=lax.Precisi...  84.4 us
    another operation x2, local copies, waits for them, and re-layouts, hadamard(): view = block3.reshape(lead * done, factor, length // (done * factor) * tail)  30.5 us
    all_to_all x2, local copies, waits for them, and re-layouts, on_device(): lax.all_to_all(mixed, 'param', split_axis=1, concat_axis=0, tiled=True)  25.8 us
    all_gather x1, waiting for transfers between devices, on_device(): all_stacked = lax.all_gather(stacked, 'doc', axis=0, tiled=True)  23.2 us
  transfers between devices with their start and end apart: 3, of which 3 were waited for; matrix products, arithmetic and copies ran while one was open for 0% of the time, Pallas kernels for 0%

commit v1 on v0

v1 whole, which is shorter than its diff:
```python
import functools

import jax
import jax.numpy as jnp
from jax import lax
from jax.experimental import pallas as pl
from jax.experimental.pallas import tpu as pltpu
from jax.sharding import PartitionSpec as P

MESH = pl.DeviceIdType.MESH
F32, BF16, I32 = jnp.float32, jnp.bfloat16, jnp.int32

WAITS = [
    [(0, 1, 0), (0, 3, 0), (1, 0, 1), (1, 0, 3)],
    [(0, 0, 1), (0, 0, 3), (1, 1, 0), (1, 3, 0)],
    [(0, 2, 0), (1, 0, 2)],
    [(0, 1, 1), (1, 1, 1), (0, 1, 3), (1, 3, 1), (0, 3, 1), (1, 1, 3), (0, 3, 3), (1, 3, 3)],
    [(0, 0, 2), (1, 2, 0)],
    [(0, 2, 1), (1, 1, 2), (0, 2, 3), (1, 3, 2)],
    [(0, 1, 2), (1, 2, 1), (0, 3, 2), (1, 2, 3)],
    [(0, 2, 2), (1, 2, 2)],
]
PAIRS = [
    [],
    [],
    [((1, 0), (3, 0))],
    [((0, 1), (0, 3))],
    [((0, 0), (2, 0)), ((1, 1), (3, 3))],
    [((1, 3), (3, 1))],
    [((2, 1), (2, 3)), ((1, 2), (3, 2))],
    [((0, 2), (2, 2))],
]


def hops(piece, u, v):
    a, b = (u, v) if piece == 0 else (v, u)
    if (a, b) == (0, 0):
        out = [(1, 0), (3, 0), (0, 1), (0, 3)]
    elif b == 0:
        out = ([(1, 0)] if a == 1 else []) + [(0, 1), (0, 3)]
    elif b == 1:
        out = [(0, 1)]
    else:
        out = []
    return out if piece == 0 else [(d, c) for c, d in out]


def parity(t):
    for s in (8, 4, 2, 1):
        t = t ^ (t >> s)
    return t & 1


def sylvester(n):
    i = lax.broadcasted_iota(I32, (n, n), 0)
    j = lax.broadcasted_iota(I32, (n, n), 1)
    return (1 - 2 * parity(i & j)).astype(F32).astype(BF16)


def halves(t):
    hi = t.astype(BF16)
    lo = (t - hi.astype(F32)).astype(BF16)
    return hi, lo


def kernel(
    li, og, ids, sb, kr, kc, out,
    gbuf, zb, z2, xq, xtb, xto, sg, stl, sts, sgs, idall, hm, lane_v, base_v, sgn_v, base_s,
    sa0, sa1, sa2, sa3, ps, pd, r1, q2, r2,
    gs, gr, ss, sr, xs_, xr, xl, ds_, dr, ls, lt, sgss, sgr, km, s1, w1, s2, w2,
):
    d = lax.axis_index("doc")
    p = lax.axis_index("param")
    x, zh, y = p // 8, (p // 4) % 2, p % 4
    zl, c = d // 2, d % 2
    z = zh * 2 + zl
    sig = 1 - 2 * c

    def dev(ax, ay, az, ac):
        return {"doc": (az % 2) * 2 + ac, "param": ax * 8 + (az // 2) * 4 + ay}

    def near(du, dv):
        return dev((x + sig * du + 4) % 4, (y + sig * dv + 4) % 4, z, c)

    sibling = dev(x, y, z, 1 - c)
    own = x * 4 + y

    sends = []
    for t in range(8):
        a = c * 8 + t
        col = ((a // 4) * 8 + (1 - zh) * 4 + a % 4) * 256 + (1 - zl) * 128
        cp = pltpu.make_async_copy(sb.at[:, pl.ds(pl.multiple_of(col, 128), 128)], sts.at[t], ls.at[t])
        cp.start()
        sends.append(cp)
    keeps = []
    for a in range(16):
        col = ((a // 4) * 8 + zh * 4 + a % 4) * 256 + zl * 128
        keeps.append(pltpu.make_async_copy(sb.at[:, pl.ds(pl.multiple_of(col, 128), 128)], stl.at[a], lt.at[a]))

    @pl.when(c == zh)
    def _():
        for cp in keeps:
            cp.start()

    bar = pltpu.get_barrier_semaphore()
    plane = [(i, j) for i in range(4) for j in range(4) if (i, j) != (0, 0)]
    line = [(k, m) for k in range(4) for m in range(2) if (k, m) != (0, 0)]

    def mate(k, m):
        return dev(x, y, (z + k) % 4, (c + m) % 2)

    for i, j in plane:
        pl.semaphore_signal(bar, inc=1, device_id=near(i, j), device_id_type=MESH)
    for k, m in line:
        pl.semaphore_signal(bar, inc=1, device_id=mate(k, m), device_id_type=MESH)

    @pl.when(zl == 0)
    def _():
        gbuf[own, d] = og[:, :128]

    @pl.when(zl == 1)
    def _():
        gbuf[own, d] = og[:, 128:]

    idall[d] = ids[...]
    pl.semaphore_wait(bar, len(plane) + len(line))

    def remote(src, dst, s, r, to):
        return pltpu.make_async_remote_copy(
            src_ref=src, dst_ref=dst, send_sem=s, recv_sem=r, device_id=to, device_id_type=MESH
        )

    pending = []
    count = [0]

    def quarter(piece):
        return (zl if piece == 0 else 1 - zl) * 2 + c

    def slot(u, v):
        return ((x - sig * u + 4) % 4) * 4 + (y - sig * v + 4) % 4

    def pass_on(piece, u, v):
        ref = gbuf.at[slot(u, v), quarter(piece)]
        for du, dv in hops(piece, u, v):
            cp = remote(ref, ref, gs.at[count[0]], gr.at[piece, (u + du) % 4, (v + dv) % 4], near(du, dv))
            count[0] += 1
            cp.start()
            pending.append(cp)
        cp = remote(ref, ref, ss.at[piece, u, v], sr.at[piece, u, v], sibling)
        cp.start()
        pending.append(cp)

    def arrived(piece, u, v):
        ref = gbuf.at[slot(u, v), quarter(piece)]
        remote(ref, ref, ss.at[piece, u, v], gr.at[piece, u, v], sibling).wait_recv()

    ex = remote(
        og.at[:, pl.ds(pl.multiple_of((1 - zl) * 128, 128), 128)], gbuf.at[own, d], gs.at[30], gr.at[1, 0, 0],
        dev(x, y, zh * 2 + 1 - zl, c),
    )
    ex.start()
    pending.append(ex)
    pass_on(0, 0, 0)
    for i, to in enumerate([sibling, dev(x, y, zh * 2 + 1 - zl, c), dev(x, y, zh * 2 + 1 - zl, 1 - c)]):
        cp = remote(ids, idall.at[d], ds_.at[i], dr.at[d], to)
        cp.start()
        pending.append(cp)

    for k in range(1, 4):
        cp = remote(li, xq.at[d], xs_.at[k], xr.at[d], dev(x, y, (z + k) % 4, zh))
        cp.start()
        pending.append(cp)
    near_x = remote(li, xq.at[d], xs_.at[0], xr.at[d], sibling)
    own_x = pltpu.make_async_copy(li, xq.at[d], xl)

    @pl.when(c != zh)
    def _():
        near_x.start()

    @pl.when(c == zh)
    def _():
        own_x.start()

    for t in range(8):
        sends[t].wait()
        sgs[t] = (2 * sts[t] - 1).astype(F32).astype(BF16)
    cp = remote(sgs, sg.at[pl.ds(c * 8, 8)], sgss, sgr.at[c], dev(x, y, (1 - zh) * 2 + 1 - zl, zh))
    cp.start()
    pending.append(cp)

    arrived(1, 0, 0)
    pass_on(1, 0, 0)

    @pl.when(c == zh)
    def _():
        for a in range(16):
            keeps[a].wait()
            sg[a] = (2 * stl[a] - 1).astype(F32).astype(BF16)

    rows, cols = kr[...], kc[...]
    base_v[...] = (((cols >> 11) & 3) * 4 + ((cols >> 8) & 3)) * 256 + (rows & 255)
    lane_v[...] = cols & 127
    rmask = x * 2048 + c * 1024 + y * 256
    cmask = zh * 1024 + zl * 128
    bits = parity((rows & rmask) ^ (cols & cmask))
    sgn_v[...] = (1 - 2 * bits).astype(F32) * (1.0 / 8192)
    to_s = pltpu.make_async_copy(base_v, base_s, km)
    to_s.start()
    hm[...] = sylvester(256)

    def service(step):
        for piece, u, v in WAITS[step]:
            arrived(piece, u, v)
            pass_on(piece, u, v)

    def prepare():
        for q in range(4):
            got = remote(li, xq.at[q], xs_.at[0], xr.at[q], sibling)
            mine = (d == q) & (c == zh)

            @pl.when(mine)
            def _():
                own_x.wait()

            @pl.when(jnp.logical_not(mine))
            def _():
                got.wait_recv()

            @pl.when(d != q)
            def _():
                remote(ids, idall.at[q], ds_.at[0], dr.at[q], sibling).wait_recv()

        big = idall[2][0:1, 0:1]
        for q in range(4):
            idq = idall[q][0:1, :]
            xt = xq[q].astype(F32).T
            xtb[:, q * 512:(q + 1) * 512] = jnp.where(idq == big, xt, 0.0).astype(BF16)
            if q in (0, 3):
                for o in range(3):
                    label = o + (big <= o).astype(I32)
                    col = 0 if q == 0 else 512
                    xto[o * 256:(o + 1) * 256, col:col + 512] = jnp.where(idq == label, xt, 0.0).astype(BF16)

    def pair(one, two):
        for u, v in (one, two):
            for piece in range(2):
                a, b = (-u) % 4, (-v) % 4
                qt = (zl if piece == 0 else 1 - zl) * 2 + 1 - c
                ref = gbuf.at[slot(u, v), qt]
                remote(ref, ref, ss.at[piece, a, b], sr.at[piece, a, b], sibling).wait_recv()
        sa, sb_ = slot(*one), slot(*two)
        w = jnp.concatenate([gbuf[sa].reshape(2048, 128), gbuf[sb_].reshape(2048, 128)], axis=1)
        signs = jnp.concatenate([sg[sa], sg[sb_]], axis=1).astype(F32)
        outer = jnp.concatenate([w[:512], w[1536:]], axis=0)

        for s in range(4):
            if s == 0:
                g = jnp.dot(xtb[...], w, preferred_element_type=F32)
            else:
                g = jnp.dot(xto[(s - 1) * 256:s * 256, :], outer, preferred_element_type=F32)
            hi, lo = halves(g * signs)
            t = jnp.dot(hm[...], hi, preferred_element_type=F32) + jnp.dot(hm[...], lo, preferred_element_type=F32)
            zb[s, sa] = t[:, :128]
            zb[s, sb_] = t[:, 128:]

    for step in range(8):
        service(step)
        if step == 2:
            prepare()

            @pl.when(c != zh)
            def _():
                for h in range(2):
                    remote(sgs, sg.at[pl.ds(h * 8, 8)], sgss, sgr.at[h], sibling).wait_recv()

        for one, two in PAIRS[step]:
            pair(one, two)

    def fly(r, carry):
        for s in range(4):
            v = [zb[s, a, pl.ds(pl.multiple_of(r * 8, 8), 8), :] for a in range(16)]
            h = 1
            while h < 16:
                n = list(v)
                for a in range(16):
                    if a & h == 0:
                        n[a], n[a + h] = v[a] + v[a + h], v[a] - v[a + h]
                v = n
                h *= 2
            for a in range(16):
                z2[pl.ds(a * 256 + r * 8, 8), s, :] = v[a]
        return carry

    lax.fori_loop(0, 32, fly, 0)

    to_s.wait()
    stage = (sa0, sa1, sa2, sa3)
    lanes = lax.broadcasted_iota(I32, (8, 128), 1)
    sub = lax.broadcasted_iota(I32, (128, 128), 0)

    def fetch(t, g):
        for j in range(128):
            t[pl.ds(4 * j, 4), :] = z2[base_s[g, j]]

    def settle(t, g):
        h = (1 - 2 * parity(sub & lane_v[pl.ds(g, 1), :])).astype(F32).astype(BF16)
        hi, lo = halves(t[...])
        r = jnp.dot(
            jnp.concatenate([hi, lo], axis=1), jnp.concatenate([h, h], axis=0), preferred_element_type=F32
        )
        acc = [jnp.zeros((8, 128), F32) for _ in range(4)]
        for q in range(64):
            acc[q % 4] = jnp.where((lanes >> 1) == q, r[8 * q:8 * q + 8, :], acc[q % 4])
        t = (acc[0] + acc[1]) + (acc[2] + acc[3])
        t = jnp.where((lanes[:4] & 1) == 0, t[:4], t[4:])
        for s in range(4):
            ps[s, pl.ds(g, 1), :] = t[s:s + 1, :]

    def pick(i, carry):
        for n in range(4):
            fetch(stage[n], i * 4 + n)
        for n in range(4):
            settle(stage[n], i * 4 + n)
        return carry

    lax.fori_loop(0, 16, pick, 0)

    big = jnp.broadcast_to(idall[2][0:1, 0:1], (64, 128))
    sign = sgn_v[...]
    for e in range(4):
        t = jnp.where(big > e, ps[min(e + 1, 3)], ps[e])
        t = jnp.where(big == e, ps[0], t) * sign
        for h in range(2):
            for i in range(4):
                g0 = (i * 2 + h) * 8
                pd[e * 2 + h, i] = t[g0:g0 + 8, :]
    me8 = d * 2 + zh
    r1[me8] = pd[me8]
    for n, (k, m) in enumerate(line):
        tz, tc = (z + k) % 4, (c + m) % 2
        dest = ((tz % 2) * 2 + tc) * 2 + tz // 2
        cp = remote(pd.at[dest], r1.at[me8], s1.at[n], w1.at[me8], mate(k, m))
        cp.start()
        pending.append(cp)
    for k, m in line:
        tz, tc = (z + k) % 4, (c + m) % 2
        src = ((tz % 2) * 2 + tc) * 2 + tz // 2
        remote(pd.at[src], r1.at[src], s1.at[0], w1.at[src], sibling).wait_recv()
    for i in range(4):
        t = r1[0, i]
        for n in range(1, 8):
            t = t + r1[n, i]
        for j in range(4):
            q2[i * 4 + j, 0:2, :] = t[2 * j:2 * j + 2, :]
            q2[i * 4 + j, 2:8, :] = jnp.zeros((6, 128), F32)
    r2[own] = q2[own]
    for n, (i, j) in enumerate(plane):
        dest = ((x + sig * i + 4) % 4) * 4 + (y + sig * j + 4) % 4
        cp = remote(q2.at[dest], r2.at[own], s2.at[n], w2.at[own], near(i, j))
        cp.start()
        pending.append(cp)
    for i, j in plane:
        src = ((x + sig * i + 4) % 4) * 4 + (y + sig * j + 4) % 4
        remote(q2.at[src], r2.at[src], s2.at[0], w2.at[src], sibling).wait_recv()
    t = r2[0]
    for n in range(1, 16):
        t = t + r2[n]
    out[...] = t

    @pl.when(c != zh)
    def _():
        near_x.wait_send()

    for cp in pending:
        cp.wait_send()


def on_device(layer_input, output_grad, doc_ids, sign_bits, kept_rows, kept_cols):
    vm = pl.BlockSpec(memory_space=pltpu.VMEM)
    dma = pltpu.SemaphoreType.DMA
    scratch = [
        pltpu.VMEM((16, 4, 512, 128), BF16),
        pltpu.VMEM((4, 16, 256, 128), F32),
        pltpu.VMEM((4096, 4, 128), F32),
        pltpu.VMEM((4, 512, 256), BF16),
        pltpu.VMEM((256, 2048), BF16),
        pltpu.VMEM((768, 1024), BF16),
        pltpu.VMEM((16, 256, 128), BF16),
        pltpu.VMEM((16, 256, 128), I32),
        pltpu.VMEM((8, 256, 128), I32),
        pltpu.VMEM((8, 256, 128), BF16),
        pltpu.VMEM((4, 8, 512), I32),
        pltpu.VMEM((256, 256), BF16),
        pltpu.VMEM((64, 128), I32),
        pltpu.VMEM((64, 128), I32),
        pltpu.VMEM((64, 128), F32),
        pltpu.SMEM((64, 128), I32),
        pltpu.VMEM((512, 128), F32),
        pltpu.VMEM((512, 128), F32),
        pltpu.VMEM((512, 128), F32),
        pltpu.VMEM((512, 128), F32),
        pltpu.VMEM((4, 64, 128), F32),
        pltpu.VMEM((8, 4, 8, 128), F32),
        pltpu.VMEM((8, 4, 8, 128), F32),
        pltpu.VMEM((16, 8, 128), F32),
        pltpu.VMEM((16, 8, 128), F32),
        dma((31,)), dma((2, 4, 4)), dma((2, 4, 4)), dma((2, 4, 4)),
        dma((4,)), dma((4,)), dma(()), dma((3,)), dma((4,)),
        dma((8,)), dma((16,)), dma(()), dma((2,)), dma(()),
        dma((7,)), dma((8,)), dma((15,)), dma((16,)),
    ]
    got = pl.pallas_call(
        kernel,
        out_shape=jax.ShapeDtypeStruct((8, 128), F32),
        in_specs=[vm, vm, vm, pl.BlockSpec(memory_space=pl.ANY), vm, vm],
        out_specs=vm,
        scratch_shapes=scratch,
        compiler_params=pltpu.CompilerParams(
            collective_id=0, has_side_effects=True, vmem_limit_bytes=60 << 20
        ),
        name="sketch",
    )(
        layer_input, output_grad, jnp.broadcast_to(doc_ids[None, :], (8, 512)), sign_bits,
        kept_rows.reshape(64, 128), kept_cols.reshape(64, 128),
    )
    return got[:2].reshape(1, 256)


def solution(mesh):
    placed = (P("doc", "param"), P("doc", "param"), P("doc"), P("param", None), P(), P())
    return jax.shard_map(
        on_device, mesh=mesh, in_specs=placed, out_specs=P("doc", "param"), check_vma=False
    )
```

time: 995 us -> 88.2 us (0.09); the launches traced: 983 us -> 88.1 us
  waiting for transfers between devices: 458 us -> 0 us
  local copies, waits for them, and re-layouts: 208 us -> 2.51 us
  blocking collectives: 185 us -> 0 us
  matrix products: 104 us -> 0 us
  Pallas kernels: 0 us -> 85.5 us
  between operations: 16.7 us -> 0.01 us
    all_gather x2 -> x0, waiting for transfers between devices: 311 us -> none  [the longest x1 288 us: on_device(): lax.all_gather(grads_part, 'param', axis=1, tiled=True)]
    unnamed x1 -> x0, blocking collectives: 180 us -> none
    all_to_all x1 -> x0, waiting for transfers between devices: 147 us -> none  [on_device(): lax.all_to_all(mixed, 'param', split_axis=1, concat_axis=0, tiled=True)]
    dot_general x6 -> x0, matrix products: 104 us -> none  [the longest x5 84.4 us: hadamard(): jnp.einsum('afb,gf->agb', view, sign_table(factor), precision=lax.Precisi...]
    gather x1 -> x0, local copies, waits for them, and re-layouts: 96.4 us -> none  [on_device(): value = whole.reshape(-1)[flat]]
    pallas_call x0 -> x1, Pallas kernels: none -> 85.5 us  [on_device(): pl.pallas_call(kernel, out_shape=jax.ShapeDtypeStruct((8, 128), F32), in_...]
    another operation x2 -> x0, local copies, waits for them, and re-layouts: 30.5 us -> none  [hadamard(): view = block3.reshape(lead * done, factor, length // (done * factor) * tail)]
    all_to_all x2 -> x0, local copies, waits for them, and re-layouts: 25.8 us -> none  [on_device(): lax.all_to_all(mixed, 'param', split_axis=1, concat_axis=0, tiled=True)]
  transfers between devices with their start and end apart: 3 -> 0, of which waited for: 3 -> 0; matrix products, arithmetic and copies ran while one was open for 0% -> 0% of each run, Pallas kernels for 0% -> 0%
where the time goes in v1:
time: 88.2 us; the launch traced here: 88.1 us
  Pallas kernels  85.5 us (97%)
  local copies, waits for them, and re-layouts  2.51 us (3%)
    pallas_call x1, Pallas kernels, on_device(): pl.pallas_call(kernel, out_shape=jax.ShapeDtypeStruct((8, 128), F32), in_...  85.5 us

profile of v1, /device:TPU:0, one launch (start us, length us, event | category | flops | bytes accessed | tf_op | source)
XLA Modules:
  0.0 88.1 jit_solution(3139929534830210283)
XLA Ops:
  0.0 1.3 %broadcast_in_dim.2.ids = s32[8,512]{1,0:T(8,128)} broadcast(s32[512]{0:T(512)} %param.8), dimensions={1} | broadcast | bytes 18432 | tf_op jit(solution)/shard_map/broadcast_in_dim | solution.py:423
  1.3 85.5 %sketch.1 = f32[8,128]{1,0:T(8,128)} custom-call(bf16[512,256]{1,0:T(8,128)(2,1)} %li.1, bf16[512,256]{1,0:T(8,128)(2,1)} %og.1, s32[8,512]{1,0:T(8,128)} %broadcast_in_dim.2.ids, s32[256,8192]{1,0:T(8,128)} %sb.1, s32[64,128]{1,0:T(8,128)} %bitcast.3, s32[64,128]{1,0:T(8,128)} %bitcast.4), custom_call_target="tpu_custom_call" | custom-call | tf_op jit(solution)/shard_map/sketch/pallas_call | solution.py:412
  86.8 1.2 %slice.3 = f32[2,128]{1,0:T(2,128)} slice(f32[8,128]{1,0:T(8,128)} %sketch.1), slice={[0:2], [0:128]} | slice | bytes 2048 | tf_op jit(solution)/shard_map/slice | solution.py:426

commit v2 on v1

--- a/solution.py
+++ b/solution.py
@@ -12,24 +12,19 @@
 
 WAITS = [
     [(0, 1, 0), (0, 3, 0), (1, 0, 1), (1, 0, 3)],
-    [(0, 0, 1), (0, 0, 3), (1, 1, 0), (1, 3, 0)],
-    [(0, 2, 0), (1, 0, 2)],
-    [(0, 1, 1), (1, 1, 1), (0, 1, 3), (1, 3, 1), (0, 3, 1), (1, 1, 3), (0, 3, 3), (1, 3, 3)],
-    [(0, 0, 2), (1, 2, 0)],
-    [(0, 2, 1), (1, 1, 2), (0, 2, 3), (1, 3, 2)],
+    [(0, 2, 0), (1, 0, 2), (0, 0, 1), (1, 1, 0)],
+    [(0, 1, 1), (1, 1, 1), (0, 3, 1), (1, 1, 3)],
+    [(0, 2, 1), (1, 1, 2), (0, 0, 3), (1, 3, 0)],
+    [(0, 1, 3), (1, 3, 1), (0, 3, 3), (1, 3, 3)],
+    [(0, 2, 3), (1, 3, 2), (0, 0, 2), (1, 2, 0)],
     [(0, 1, 2), (1, 2, 1), (0, 3, 2), (1, 2, 3)],
     [(0, 2, 2), (1, 2, 2)],
 ]
 PAIRS = [
-    [],
-    [],
-    [((1, 0), (3, 0))],
-    [((0, 1), (0, 3))],
-    [((0, 0), (2, 0)), ((1, 1), (3, 3))],
-    [((1, 3), (3, 1))],
-    [((2, 1), (2, 3)), ((1, 2), (3, 2))],
-    [((0, 2), (2, 2))],
+    ((1, 0), (3, 0)), ((0, 1), (0, 3)), ((1, 1), (3, 3)), ((1, 3), (3, 1)),
+    ((0, 0), (2, 0)), ((2, 1), (2, 3)), ((1, 2), (3, 2)), ((0, 2), (2, 2)),
 ]
+READY = {3: (0, 1), 4: (2, 3), 5: (4,), 6: (5, 6), 7: (7,)}
 
 
 def hops(piece, u, v):
@@ -46,9 +41,9 @@
 
 
 def parity(t):
-    for s in (8, 4, 2, 1):
+    for s in (8, 4):
         t = t ^ (t >> s)
-    return t & 1
+    return (jnp.int32(0x6996) >> (t & 15)) & 1
 
 
 def sylvester(n):
@@ -65,7 +60,7 @@
 
 def kernel(
     li, og, ids, sb, kr, kc, out,
-    gbuf, zb, z2, xq, xtb, xto, sg, stl, sts, sgs, idall, hm, lane_v, base_v, sgn_v, base_s,
+    gbuf, zb, z2, xq, xtb, xto, sg, stl, sts, sgs, idall, hm, mcol, lane_v, base_v, sgn_v, base_a, base_b,
     sa0, sa1, sa2, sa3, ps, pd, r1, q2, r2,
     gs, gr, ss, sr, xs_, xr, xl, ds_, dr, ls, lt, sgss, sgr, km, s1, w1, s2, w2,
 ):
@@ -85,23 +80,6 @@
     sibling = dev(x, y, z, 1 - c)
     own = x * 4 + y
 
-    sends = []
-    for t in range(8):
-        a = c * 8 + t
-        col = ((a // 4) * 8 + (1 - zh) * 4 + a % 4) * 256 + (1 - zl) * 128
-        cp = pltpu.make_async_copy(sb.at[:, pl.ds(pl.multiple_of(col, 128), 128)], sts.at[t], ls.at[t])
-        cp.start()
-        sends.append(cp)
-    keeps = []
-    for a in range(16):
-        col = ((a // 4) * 8 + zh * 4 + a % 4) * 256 + zl * 128
-        keeps.append(pltpu.make_async_copy(sb.at[:, pl.ds(pl.multiple_of(col, 128), 128)], stl.at[a], lt.at[a]))
-
-    @pl.when(c == zh)
-    def _():
-        for cp in keeps:
-            cp.start()
-
     bar = pltpu.get_barrier_semaphore()
     plane = [(i, j) for i in range(4) for j in range(4) if (i, j) != (0, 0)]
     line = [(k, m) for k in range(4) for m in range(2) if (k, m) != (0, 0)]
@@ -113,6 +91,28 @@
         pl.semaphore_signal(bar, inc=1, device_id=near(i, j), device_id_type=MESH)
     for k, m in line:
         pl.semaphore_signal(bar, inc=1, device_id=mate(k, m), device_id_type=MESH)
+
+    def column(a, h, l):
+        return pl.multiple_of(((a // 4) * 8 + h * 4 + a % 4) * 256 + l * 128, 128)
+
+    def far_slot(u, v):
+        f = 1 - 2 * zh
+        return ((x - f * u + 4) % 4) * 4 + (y - f * v + 4) % 4
+
+    sends = []
+    for t in range(8):
+        a = jnp.where(c == 0, far_slot(*PAIRS[t][0]), far_slot(*PAIRS[t][1]))
+        cp = pltpu.make_async_copy(sb.at[:, pl.ds(column(a, 1 - zh, 1 - zl), 128)], sts.at[t], ls.at[t])
+        cp.start()
+        sends.append((a, cp))
+    keeps = []
+    for a in range(16):
+        keeps.append(pltpu.make_async_copy(sb.at[:, pl.ds(column(a, zh, zl), 128)], stl.at[a], lt.at[a]))
+
+    @pl.when(c == zh)
+    def _():
+        for cp in keeps:
+            cp.start()
 
     @pl.when(zl == 0)
     def _():
@@ -166,10 +166,11 @@
         cp.start()
         pending.append(cp)
 
-    for k in range(1, 4):
-        cp = remote(li, xq.at[d], xs_.at[k], xr.at[d], dev(x, y, (z + k) % 4, zh))
-        cp.start()
-        pending.append(cp)
+    beside, across = zh * 2 + 1 - zl, (1 - zh) * 2 + 1 - zl
+    x_over = remote(li, xq.at[d], xs_.at[2], xr.at[d], dev(x, y, across, zh))
+    x_over.start()
+    x_side = remote(li, xq.at[d], xs_.at[1], xr.at[d], dev(x, y, beside, zh))
+    x_side.start()
     near_x = remote(li, xq.at[d], xs_.at[0], xr.at[d], sibling)
     own_x = pltpu.make_async_copy(li, xq.at[d], xl)
 
@@ -181,12 +182,26 @@
     def _():
         own_x.start()
 
+    relays = []
+    for k in range(2):
+        ref = xq.at[(1 - zl) * 2 + k]
+        relays.append(remote(ref, ref, xs_.at[3 + k], xr.at[(1 - zl) * 2 + k], dev(x, y, beside, c)))
+
     for t in range(8):
-        sends[t].wait()
+        sends[t][1].wait()
         sgs[t] = (2 * sts[t] - 1).astype(F32).astype(BF16)
-    cp = remote(sgs, sg.at[pl.ds(c * 8, 8)], sgss, sgr.at[c], dev(x, y, (1 - zh) * 2 + 1 - zl, zh))
-    cp.start()
-    pending.append(cp)
+
+    def send_signs():
+        for k in range(2):
+            @pl.when(c != zh)
+            def _():
+                relays[k].wait_recv()
+                relays[k].start()
+        x_over.wait_send()
+        for t in range(8):
+            cp = remote(sgs.at[t], sg.at[sends[t][0]], sgss.at[t], sgr.at[t, c], dev(x, y, across, zh))
+            cp.start()
+            pending.append(cp)
 
     arrived(1, 0, 0)
     pass_on(1, 0, 0)
@@ -198,14 +213,20 @@
             sg[a] = (2 * stl[a] - 1).astype(F32).astype(BF16)
 
     rows, cols = kr[...], kc[...]
-    base_v[...] = (((cols >> 11) & 3) * 4 + ((cols >> 8) & 3)) * 256 + (rows & 255)
+    base_v[...] = ((((cols >> 11) & 3) * 4 + ((cols >> 8) & 3)) * 256 + (rows & 255)) * 4
     lane_v[...] = cols & 127
     rmask = x * 2048 + c * 1024 + y * 256
     cmask = zh * 1024 + zl * 128
     bits = parity((rows & rmask) ^ (cols & cmask))
     sgn_v[...] = (1 - 2 * bits).astype(F32) * (1.0 / 8192)
-    to_s = pltpu.make_async_copy(base_v, base_s, km)
-    to_s.start()
+    def index_a(i):
+        return pltpu.make_async_copy(base_v.at[i], base_a, km.at[0])
+
+    def index_b(i):
+        return pltpu.make_async_copy(base_v.at[i], base_b, km.at[1])
+
+    index_a(0).start()
+    index_b(1).start()
     hm[...] = sylvester(256)
 
     def service(step):
@@ -217,12 +238,13 @@
         for q in range(4):
             got = remote(li, xq.at[q], xs_.at[0], xr.at[q], sibling)
             mine = (d == q) & (c == zh)
+            seen = (c != zh) & ((q // 2) != zl)
 
             @pl.when(mine)
             def _():
                 own_x.wait()
 
-            @pl.when(jnp.logical_not(mine))
+            @pl.when(jnp.logical_not(mine | seen))
             def _():
                 got.wait_recv()
 
@@ -230,18 +252,25 @@
             def _():
                 remote(ids, idall.at[q], ds_.at[0], dr.at[q], sibling).wait_recv()
 
-        big = idall[2][0:1, 0:1]
-        for q in range(4):
-            idq = idall[q][0:1, :]
-            xt = xq[q].astype(F32).T
-            xtb[:, q * 512:(q + 1) * 512] = jnp.where(idq == big, xt, 0.0).astype(BF16)
-            if q in (0, 3):
-                for o in range(3):
-                    label = o + (big <= o).astype(I32)
-                    col = 0 if q == 0 else 512
-                    xto[o * 256:(o + 1) * 256, col:col + 512] = jnp.where(idq == label, xt, 0.0).astype(BF16)
-
-    def pair(one, two):
+        def labels(q):
+            return jnp.concatenate([idall[q, i:i + 1, :] for i in range(4)], axis=1)
+
+        big = idall[2, 0:1, 0:1]
+        id0, id3 = labels(0), labels(3)
+        short = id0 != big
+        x0, x3 = xq[0].astype(F32).T, xq[3].astype(F32).T
+        xtb[:, 0:512] = xq[1].astype(F32).T.astype(BF16)
+        xtb[:, 512:1024] = xq[2].astype(F32).T.astype(BF16)
+        xtb[:, 1024:1536] = jnp.where(short, x3, x0).astype(BF16)
+        rest, id_rest = jnp.where(short, x0, x3), jnp.where(short, id0, id3)
+        for o in range(3):
+            label = o + (big <= o).astype(I32)
+            xto[o * 256:(o + 1) * 256, :] = jnp.where(id_rest == label, rest, 0.0).astype(BF16)
+        side = jnp.broadcast_to(short.astype(F32), (128, 512)).T.astype(BF16)
+        mcol[...] = jnp.concatenate([side, side], axis=1)
+
+    def pair(n):
+        one, two = PAIRS[n]
         for u, v in (one, two):
             for piece in range(2):
                 a, b = (-u) % 4, (-v) % 4
@@ -249,15 +278,20 @@
                 ref = gbuf.at[slot(u, v), qt]
                 remote(ref, ref, ss.at[piece, a, b], sr.at[piece, a, b], sibling).wait_recv()
         sa, sb_ = slot(*one), slot(*two)
-        w = jnp.concatenate([gbuf[sa].reshape(2048, 128), gbuf[sb_].reshape(2048, 128)], axis=1)
+
+        @pl.when(c != zh)
+        def _():
+            for h, a in enumerate((sa, sb_)):
+                remote(sgs.at[0], sg.at[a], sgss.at[0], sgr.at[n, h], sibling).wait_recv()
+
+        w = [jnp.concatenate([gbuf[sa, q], gbuf[sb_, q]], axis=1) for q in range(4)]
         signs = jnp.concatenate([sg[sa], sg[sb_]], axis=1).astype(F32)
-        outer = jnp.concatenate([w[:512], w[1536:]], axis=0)
-
+        short = mcol[...] != 0
+        long_w = jnp.concatenate([w[1], w[2], jnp.where(short, w[3], w[0])], axis=0)
+        g0 = jnp.dot(xtb[...], long_w, preferred_element_type=F32)
+        g1 = jnp.dot(xto[...], jnp.where(short, w[0], w[3]), preferred_element_type=F32)
         for s in range(4):
-            if s == 0:
-                g = jnp.dot(xtb[...], w, preferred_element_type=F32)
-            else:
-                g = jnp.dot(xto[(s - 1) * 256:s * 256, :], outer, preferred_element_type=F32)
+            g = g0 if s == 0 else g1[(s - 1) * 256:s * 256]
             hi, lo = halves(g * signs)
             t = jnp.dot(hm[...], hi, preferred_element_type=F32) + jnp.dot(hm[...], lo, preferred_element_type=F32)
             zb[s, sa] = t[:, :128]
@@ -265,16 +299,12 @@
 
     for step in range(8):
         service(step)
-        if step == 2:
+        if step == 1:
+            send_signs()
+        if step == 3:
             prepare()
-
-            @pl.when(c != zh)
-            def _():
-                for h in range(2):
-                    remote(sgs, sg.at[pl.ds(h * 8, 8)], sgss, sgr.at[h], sibling).wait_recv()
-
-        for one, two in PAIRS[step]:
-            pair(one, two)
+        for n in READY.get(step, ()):
+            pair(n)
 
     def fly(r, carry):
         for s in range(4):
@@ -288,22 +318,21 @@
                 v = n
                 h *= 2
             for a in range(16):
-                z2[pl.ds(a * 256 + r * 8, 8), s, :] = v[a]
+                z2[pl.ds(a * 1024 + r * 32 + s, 8, stride=4), :] = v[a]
         return carry
 
     lax.fori_loop(0, 32, fly, 0)
 
-    to_s.wait()
     stage = (sa0, sa1, sa2, sa3)
     lanes = lax.broadcasted_iota(I32, (8, 128), 1)
     sub = lax.broadcasted_iota(I32, (128, 128), 0)
 
-    def fetch(t, g):
+    def fetch(t, base, n):
         for j in range(128):
-            t[pl.ds(4 * j, 4), :] = z2[base_s[g, j]]
-
-    def settle(t, g):
-        h = (1 - 2 * parity(sub & lane_v[pl.ds(g, 1), :])).astype(F32).astype(BF16)
+            t[pl.ds(4 * j, 4), :] = z2[pl.ds(base[n, j], 4), :]
+
+    def settle(t, i, n):
+        h = jnp.where(parity(sub & lane_v[i, n:n + 1, :]) == 1, -1.0, 1.0).astype(BF16)
         hi, lo = halves(t[...])
         r = jnp.dot(
             jnp.concatenate([hi, lo], axis=1), jnp.concatenate([h, h], axis=0), preferred_element_type=F32
@@ -314,26 +343,32 @@
         t = (acc[0] + acc[1]) + (acc[2] + acc[3])
         t = jnp.where((lanes[:4] & 1) == 0, t[:4], t[4:])
         for s in range(4):
-            ps[s, pl.ds(g, 1), :] = t[s:s + 1, :]
+            ps[s, i, n:n + 1, :] = t[s:s + 1, :]
 
     def pick(i, carry):
-        for n in range(4):
-            fetch(stage[n], i * 4 + n)
-        for n in range(4):
-            settle(stage[n], i * 4 + n)
+        for k, (index, base) in enumerate(((index_a, base_a), (index_b, base_b))):
+            m = 2 * i + k
+            index(m).wait()
+            for n in range(4):
+                fetch(stage[n], base, n)
+            index(jnp.minimum(m + 2, 15)).start()
+            for n in range(4):
+                settle(stage[n], m, n)
         return carry
 
-    lax.fori_loop(0, 16, pick, 0)
-
-    big = jnp.broadcast_to(idall[2][0:1, 0:1], (64, 128))
+    lax.fori_loop(0, 8, pick, 0)
+    index_a(0).wait()
+    index_b(0).wait()
+
+    big = jnp.broadcast_to(idall[2, 0:1, 0:1], (16, 4, 128))
     sign = sgn_v[...]
     for e in range(4):
         t = jnp.where(big > e, ps[min(e + 1, 3)], ps[e])
         t = jnp.where(big == e, ps[0], t) * sign
         for h in range(2):
             for i in range(4):
-                g0 = (i * 2 + h) * 8
-                pd[e * 2 + h, i] = t[g0:g0 + 8, :]
+                pd[e * 2 + h, i, 0:4] = t[i * 4 + h * 2]
+                pd[e * 2 + h, i, 4:8] = t[i * 4 + h * 2 + 1]
     me8 = d * 2 + zh
     r1[me8] = pd[me8]
     for n, (k, m) in enumerate(line):
@@ -370,7 +405,10 @@
     @pl.when(c != zh)
     def _():
         near_x.wait_send()
-
+        for cp in relays:
+            cp.wait_send()
+
+    x_side.wait_send()
     for cp in pending:
         cp.wait_send()
 
@@ -381,32 +419,34 @@
     scratch = [
         pltpu.VMEM((16, 4, 512, 128), BF16),
         pltpu.VMEM((4, 16, 256, 128), F32),
-        pltpu.VMEM((4096, 4, 128), F32),
+        pltpu.VMEM((16384, 128), F32),
         pltpu.VMEM((4, 512, 256), BF16),
-        pltpu.VMEM((256, 2048), BF16),
-        pltpu.VMEM((768, 1024), BF16),
+        pltpu.VMEM((256, 1536), BF16),
+        pltpu.VMEM((768, 512), BF16),
         pltpu.VMEM((16, 256, 128), BF16),
         pltpu.VMEM((16, 256, 128), I32),
         pltpu.VMEM((8, 256, 128), I32),
         pltpu.VMEM((8, 256, 128), BF16),
-        pltpu.VMEM((4, 8, 512), I32),
+        pltpu.VMEM((4, 4, 128), I32),
         pltpu.VMEM((256, 256), BF16),
-        pltpu.VMEM((64, 128), I32),
-        pltpu.VMEM((64, 128), I32),
-        pltpu.VMEM((64, 128), F32),
-        pltpu.SMEM((64, 128), I32),
+        pltpu.VMEM((512, 256), BF16),
+        pltpu.VMEM((16, 4, 128), I32),
+        pltpu.VMEM((16, 4, 128), I32),
+        pltpu.VMEM((16, 4, 128), F32),
+        pltpu.SMEM((4, 128), I32),
+        pltpu.SMEM((4, 128), I32),
         pltpu.VMEM((512, 128), F32),
         pltpu.VMEM((512, 128), F32),
         pltpu.VMEM((512, 128), F32),
         pltpu.VMEM((512, 128), F32),
-        pltpu.VMEM((4, 64, 128), F32),
+        pltpu.VMEM((4, 16, 4, 128), F32),
         pltpu.VMEM((8, 4, 8, 128), F32),
         pltpu.VMEM((8, 4, 8, 128), F32),
         pltpu.VMEM((16, 8, 128), F32),
         pltpu.VMEM((16, 8, 128), F32),
         dma((31,)), dma((2, 4, 4)), dma((2, 4, 4)), dma((2, 4, 4)),
-        dma((4,)), dma((4,)), dma(()), dma((3,)), dma((4,)),
-        dma((8,)), dma((16,)), dma(()), dma((2,)), dma(()),
+        dma((5,)), dma((4,)), dma(()), dma((3,)), dma((4,)),
+        dma((8,)), dma((16,)), dma((8,)), dma((8, 2)), dma((2,)),
         dma((7,)), dma((8,)), dma((15,)), dma((16,)),
     ]
     got = pl.pallas_call(
@@ -420,8 +460,8 @@
         ),
         name="sketch",
     )(
-        layer_input, output_grad, jnp.broadcast_to(doc_ids[None, :], (8, 512)), sign_bits,
-        kept_rows.reshape(64, 128), kept_cols.reshape(64, 128),
+        layer_input, output_grad, doc_ids.reshape(4, 128), sign_bits,
+        kept_rows.reshape(16, 4, 128), kept_cols.reshape(16, 4, 128),
     )
     return got[:2].reshape(1, 256)
 

time: 88.2 us -> 73.4 us (0.83)
  Pallas kernels: 85.5 us -> 71.9 us
  local copies, waits for them, and re-layouts: 2.51 us -> 1.25 us
    pallas_call x1, Pallas kernels: 85.5 us -> 71.9 us  [on_device(): pl.pallas_call(kernel, out_shape=jax.ShapeDtypeStruct((8, 128), F32), in_...]
    broadcast_in_dim x1 -> x0, local copies, waits for them, and re-layouts: 1.28 us -> none  [on_device(): jnp.broadcast_to(doc_ids[None, :], (8, 512))]
where the time goes in v2:
time: 73.4 us; the launch traced here: 73.1 us
  Pallas kernels  71.9 us (98%)
  local copies, waits for them, and re-layouts  1.25 us (2%)
    pallas_call x1, Pallas kernels, on_device(): pl.pallas_call(kernel, out_shape=jax.ShapeDtypeStruct((8, 128), F32), in_...  71.9 us

profile of v2, /device:TPU:0, one launch (start us, length us, event | category | flops | bytes accessed | tf_op | source)
XLA Modules:
  0.0 73.1 jit_solution(17527838418074211035)
XLA Ops:
  0.0 71.9 %sketch.1 = f32[8,128]{1,0:T(8,128)} custom-call(bf16[512,256]{1,0:T(8,128)(2,1)} %li.1, bf16[512,256]{1,0:T(8,128)(2,1)} %og.1, s32[4,128]{1,0:T(4,128)} %bitcast.6, s32[256,8192]{1,0:T(8,128)} %sb.1, s32[16,4,128]{2,1,0:T(4,128)} %bitcast.4, s32[16,4,128]{2,1,0:T(4,128)} %bitcast.5), custom_call_target="tpu_custom_call" | custom-call | tf_op jit(solution)/shard_map/sketch/pallas_call | solution.py:452
  71.9 1.2 %slice.3 = f32[2,128]{1,0:T(2,128)} slice(f32[8,128]{1,0:T(8,128)} %sketch.1), slice={[0:2], [0:128]} | slice | bytes 2048 | tf_op jit(solution)/shard_map/slice | solution.py:466

commit v3 on v2

--- a/solution.py
+++ b/solution.py
@@ -10,21 +10,16 @@
 MESH = pl.DeviceIdType.MESH
 F32, BF16, I32 = jnp.float32, jnp.bfloat16, jnp.int32
 
-WAITS = [
-    [(0, 1, 0), (0, 3, 0), (1, 0, 1), (1, 0, 3)],
-    [(0, 2, 0), (1, 0, 2), (0, 0, 1), (1, 1, 0)],
-    [(0, 1, 1), (1, 1, 1), (0, 3, 1), (1, 1, 3)],
-    [(0, 2, 1), (1, 1, 2), (0, 0, 3), (1, 3, 0)],
-    [(0, 1, 3), (1, 3, 1), (0, 3, 3), (1, 3, 3)],
-    [(0, 2, 3), (1, 3, 2), (0, 0, 2), (1, 2, 0)],
-    [(0, 1, 2), (1, 2, 1), (0, 3, 2), (1, 2, 3)],
-    [(0, 2, 2), (1, 2, 2)],
-]
 PAIRS = [
     ((1, 0), (3, 0)), ((0, 1), (0, 3)), ((1, 1), (3, 3)), ((1, 3), (3, 1)),
     ((0, 0), (2, 0)), ((2, 1), (2, 3)), ((1, 2), (3, 2)), ((0, 2), (2, 2)),
 ]
-READY = {3: (0, 1), 4: (2, 3), 5: (4,), 6: (5, 6), 7: (7,)}
+OPS = [
+    (1, 0, 0), (0, 1, 0), (0, 3, 0), "relay", (1, 0, 1), (1, 0, 3), "signs", (0, 2, 0), (1, 0, 2), (0, 0, 1),
+    (1, 1, 0), (0, 1, 1), (1, 1, 1), (0, 3, 1), (1, 1, 3), (0, 0, 3), (1, 3, 0), "inputs", 0, 1, (0, 2, 1), (1, 1, 2),
+    (0, 1, 3), (1, 3, 1), (0, 3, 3), (1, 3, 3), 2, 3, (0, 2, 3), (1, 3, 2), (0, 0, 2), (1, 2, 0), 4, (0, 1, 2),
+    (1, 2, 1), (0, 3, 2), (1, 2, 3), 5, 6, (0, 2, 2), (1, 2, 2), 7,
+]
 
 
 def hops(piece, u, v):
@@ -60,9 +55,9 @@
 
 def kernel(
     li, og, ids, sb, kr, kc, out,
-    gbuf, zb, z2, xq, xtb, xto, sg, stl, sts, sgs, idall, hm, mcol, lane_v, base_v, sgn_v, base_a, base_b,
-    sa0, sa1, sa2, sa3, ps, pd, r1, q2, r2,
-    gs, gr, ss, sr, xs_, xr, xl, ds_, dr, ls, lt, sgss, sgr, km, s1, w1, s2, w2,
+    kr_v, kc_v, gbuf, zb, z2, xq, xtb, xto, sg, stl, sts, sgs, idall, hm, mcol, lane_v, base_v, sgn_v, base_a, base_b,
+    sa0, sa1, sa2, sa3, sa4, sa5, sa6, sa7, ps, pd, r1, q2, r2,
+    lo_, gs, gr, ss, sr, xs_, xr, xl, ds_, dr, ls, lt, sgss, sgr, km, s1, w1, s2, w2,
 ):
     d = lax.axis_index("doc")
     p = lax.axis_index("param")
@@ -82,15 +77,26 @@
 
     bar = pltpu.get_barrier_semaphore()
     plane = [(i, j) for i in range(4) for j in range(4) if (i, j) != (0, 0)]
+    ring = [(1, 0), (3, 0), (0, 1), (0, 3)]
     line = [(k, m) for k in range(4) for m in range(2) if (k, m) != (0, 0)]
 
     def mate(k, m):
         return dev(x, y, (z + k) % 4, (c + m) % 2)
 
-    for i, j in plane:
+    for i, j in ring:
         pl.semaphore_signal(bar, inc=1, device_id=near(i, j), device_id_type=MESH)
     for k, m in line:
         pl.semaphore_signal(bar, inc=1, device_id=mate(k, m), device_id_type=MESH)
+
+    def half(l):
+        return og.at[:, pl.ds(pl.multiple_of(l * 128, 128), 128)]
+
+    own_g = pltpu.make_async_copy(half(zl), gbuf.at[own, d], lo_.at[0])
+    own_i = pltpu.make_async_copy(ids, idall.at[d], lo_.at[1])
+    own_r = pltpu.make_async_copy(kr, kr_v, lo_.at[2])
+    own_c = pltpu.make_async_copy(kc, kc_v, lo_.at[3])
+    for cp in (own_g, own_i, own_r, own_c):
+        cp.start()
 
     def column(a, h, l):
         return pl.multiple_of(((a // 4) * 8 + h * 4 + a % 4) * 256 + l * 128, 128)
@@ -114,16 +120,7 @@
         for cp in keeps:
             cp.start()
 
-    @pl.when(zl == 0)
-    def _():
-        gbuf[own, d] = og[:, :128]
-
-    @pl.when(zl == 1)
-    def _():
-        gbuf[own, d] = og[:, 128:]
-
-    idall[d] = ids[...]
-    pl.semaphore_wait(bar, len(plane) + len(line))
+    pl.semaphore_wait(bar, len(ring) + len(line))
 
     def remote(src, dst, s, r, to):
         return pltpu.make_async_remote_copy(
@@ -141,12 +138,13 @@
 
     def pass_on(piece, u, v):
         ref = gbuf.at[slot(u, v), quarter(piece)]
+        src = half(zl) if (piece, u, v) == (0, 0, 0) else ref
         for du, dv in hops(piece, u, v):
-            cp = remote(ref, ref, gs.at[count[0]], gr.at[piece, (u + du) % 4, (v + dv) % 4], near(du, dv))
+            cp = remote(src, ref, gs.at[count[0]], gr.at[piece, (u + du) % 4, (v + dv) % 4], near(du, dv))
             count[0] += 1
             cp.start()
             pending.append(cp)
-        cp = remote(ref, ref, ss.at[piece, u, v], sr.at[piece, u, v], sibling)
+        cp = remote(src, ref, ss.at[piece, u, v], sr.at[piece, u, v], sibling)
         cp.start()
         pending.append(cp)
 
@@ -155,7 +153,7 @@
         remote(ref, ref, ss.at[piece, u, v], gr.at[piece, u, v], sibling).wait_recv()
 
     ex = remote(
-        og.at[:, pl.ds(pl.multiple_of((1 - zl) * 128, 128), 128)], gbuf.at[own, d], gs.at[30], gr.at[1, 0, 0],
+        half(1 - zl), gbuf.at[own, d], gs.at[30], gr.at[1, 0, 0],
         dev(x, y, zh * 2 + 1 - zl, c),
     )
     ex.start()
@@ -191,20 +189,19 @@
         sends[t][1].wait()
         sgs[t] = (2 * sts[t] - 1).astype(F32).astype(BF16)
 
-    def send_signs():
+    def relay():
         for k in range(2):
             @pl.when(c != zh)
             def _():
                 relays[k].wait_recv()
                 relays[k].start()
-        x_over.wait_send()
+
+    def send_signs():
         for t in range(8):
             cp = remote(sgs.at[t], sg.at[sends[t][0]], sgss.at[t], sgr.at[t, c], dev(x, y, across, zh))
             cp.start()
             pending.append(cp)
 
-    arrived(1, 0, 0)
-    pass_on(1, 0, 0)
 
     @pl.when(c == zh)
     def _():
@@ -212,7 +209,9 @@
             keeps[a].wait()
             sg[a] = (2 * stl[a] - 1).astype(F32).astype(BF16)
 
-    rows, cols = kr[...], kc[...]
+    own_r.wait()
+    own_c.wait()
+    rows, cols = kr_v[...], kc_v[...]
     base_v[...] = ((((cols >> 11) & 3) * 4 + ((cols >> 8) & 3)) * 256 + (rows & 255)) * 4
     lane_v[...] = cols & 127
     rmask = x * 2048 + c * 1024 + y * 256
@@ -229,11 +228,6 @@
     index_b(1).start()
     hm[...] = sylvester(256)
 
-    def service(step):
-        for piece, u, v in WAITS[step]:
-            arrived(piece, u, v)
-            pass_on(piece, u, v)
-
     def prepare():
         for q in range(4):
             got = remote(li, xq.at[q], xs_.at[0], xr.at[q], sibling)
@@ -247,6 +241,10 @@
             @pl.when(jnp.logical_not(mine | seen))
             def _():
                 got.wait_recv()
+
+            @pl.when(d == q)
+            def _():
+                own_i.wait()
 
             @pl.when(d != q)
             def _():
@@ -297,14 +295,19 @@
             zb[s, sa] = t[:, :128]
             zb[s, sb_] = t[:, 128:]
 
-    for step in range(8):
-        service(step)
-        if step == 1:
+    own_g.wait()
+    for op in OPS:
+        if op == "signs":
             send_signs()
-        if step == 3:
+        elif op == "relay":
+            relay()
+        elif op == "inputs":
             prepare()
-        for n in READY.get(step, ()):
-            pair(n)
+        elif isinstance(op, int):
+            pair(op)
+        else:
+            arrived(*op)
+            pass_on(*op)
 
     def fly(r, carry):
         for s in range(4):
@@ -323,7 +326,7 @@
 
     lax.fori_loop(0, 32, fly, 0)
 
-    stage = (sa0, sa1, sa2, sa3)
+    stage = (sa0, sa1, sa2, sa3, sa4, sa5, sa6, sa7)
     lanes = lax.broadcasted_iota(I32, (8, 128), 1)
     sub = lax.broadcasted_iota(I32, (128, 128), 0)
 
@@ -345,20 +348,28 @@
         for s in range(4):
             ps[s, i, n:n + 1, :] = t[s:s + 1, :]
 
+    def round_(new, index, base, m, old):
+        index(m).wait()
+        for n in range(4):
+            fetch(new[n], base, n)
+            if old is not None:
+                settle(old[n], m - 1, n)
+        index(jnp.minimum(m + 2, 15)).start()
+
     def pick(i, carry):
-        for k, (index, base) in enumerate(((index_a, base_a), (index_b, base_b))):
-            m = 2 * i + k
-            index(m).wait()
-            for n in range(4):
-                fetch(stage[n], base, n)
-            index(jnp.minimum(m + 2, 15)).start()
-            for n in range(4):
-                settle(stage[n], m, n)
+        round_(stage[4:], index_b, base_b, 2 * i + 1, stage[:4])
+        round_(stage[:4], index_a, base_a, 2 * i + 2, stage[4:])
         return carry
 
-    lax.fori_loop(0, 8, pick, 0)
+    round_(stage[:4], index_a, base_a, 0, None)
+    lax.fori_loop(0, 7, pick, 0)
+    index_b(15).wait()
+    for n in range(4):
+        fetch(stage[4 + n], base_b, n)
+        settle(stage[n], 14, n)
+    for n in range(4):
+        settle(stage[4 + n], 15, n)
     index_a(0).wait()
-    index_b(0).wait()
 
     big = jnp.broadcast_to(idall[2, 0:1, 0:1], (16, 4, 128))
     sign = sgn_v[...]
@@ -409,6 +420,7 @@
             cp.wait_send()
 
     x_side.wait_send()
+    x_over.wait_send()
     for cp in pending:
         cp.wait_send()
 
@@ -417,6 +429,8 @@
     vm = pl.BlockSpec(memory_space=pltpu.VMEM)
     dma = pltpu.SemaphoreType.DMA
     scratch = [
+        pltpu.VMEM((16, 4, 128), I32),
+        pltpu.VMEM((16, 4, 128), I32),
         pltpu.VMEM((16, 4, 512, 128), BF16),
         pltpu.VMEM((4, 16, 256, 128), F32),
         pltpu.VMEM((16384, 128), F32),
@@ -439,12 +453,16 @@
         pltpu.VMEM((512, 128), F32),
         pltpu.VMEM((512, 128), F32),
         pltpu.VMEM((512, 128), F32),
+        pltpu.VMEM((512, 128), F32),
+        pltpu.VMEM((512, 128), F32),
+        pltpu.VMEM((512, 128), F32),
+        pltpu.VMEM((512, 128), F32),
         pltpu.VMEM((4, 16, 4, 128), F32),
         pltpu.VMEM((8, 4, 8, 128), F32),
         pltpu.VMEM((8, 4, 8, 128), F32),
         pltpu.VMEM((16, 8, 128), F32),
         pltpu.VMEM((16, 8, 128), F32),
-        dma((31,)), dma((2, 4, 4)), dma((2, 4, 4)), dma((2, 4, 4)),
+        dma((4,)), dma((31,)), dma((2, 4, 4)), dma((2, 4, 4)), dma((2, 4, 4)),
         dma((5,)), dma((4,)), dma(()), dma((3,)), dma((4,)),
         dma((8,)), dma((16,)), dma((8,)), dma((8, 2)), dma((2,)),
         dma((7,)), dma((8,)), dma((15,)), dma((16,)),
@@ -452,7 +470,7 @@
     got = pl.pallas_call(
         kernel,
         out_shape=jax.ShapeDtypeStruct((8, 128), F32),
-        in_specs=[vm, vm, vm, pl.BlockSpec(memory_space=pl.ANY), vm, vm],
+        in_specs=[pl.BlockSpec(memory_space=pl.ANY)] * 6,
         out_specs=vm,
         scratch_shapes=scratch,
         compiler_params=pltpu.CompilerParams(

time: 73.4 us -> 66.6 us (0.907)
  Pallas kernels: 71.9 us -> 65.2 us
    pallas_call x1, Pallas kernels: 71.9 us -> 65.2 us  [on_device(): pl.pallas_call(kernel, out_shape=jax.ShapeDtypeStruct((8, 128), F32), in_...]
where the time goes in v3:
time: 66.6 us; the launch traced here: 66.4 us
  Pallas kernels  65.2 us (98%)
  local copies, waits for them, and re-layouts  1.25 us (2%)
    pallas_call x1, Pallas kernels, on_device(): pl.pallas_call(kernel, out_shape=jax.ShapeDtypeStruct((8, 128), F32), in_...  65.2 us

profile of v3, /device:TPU:0, one launch (start us, length us, event | category | flops | bytes accessed | tf_op | source)
XLA Modules:
  0.0 66.4 jit_solution(1415863997928994380)
XLA Ops:
  0.0 65.2 %sketch.1 = f32[8,128]{1,0:T(8,128)} custom-call(bf16[512,256]{1,0:T(8,128)(2,1)} %li.1, bf16[512,256]{1,0:T(8,128)(2,1)} %og.1, s32[4,128]{1,0:T(4,128)} %bitcast.6, s32[256,8192]{1,0:T(8,128)} %sb.1, s32[16,4,128]{2,1,0:T(4,128)} %bitcast.4, s32[16,4,128]{2,1,0:T(4,128)} %bitcast.5), custom_call_target="tpu_custom_call" | custom-call | tf_op jit(solution)/shard_map/sketch/pallas_call | solution.py:470
  65.2 1.2 %slice.3 = f32[2,128]{1,0:T(2,128)} slice(f32[8,128]{1,0:T(8,128)} %sketch.1), slice={[0:2], [0:128]} | slice | bytes 2048 | tf_op jit(solution)/shard_map/slice | solution.py:484

commit v4 on v3

--- a/solution.py
+++ b/solution.py
@@ -16,9 +16,9 @@
 ]
 OPS = [
     (1, 0, 0), (0, 1, 0), (0, 3, 0), "relay", (1, 0, 1), (1, 0, 3), "signs", (0, 2, 0), (1, 0, 2), (0, 0, 1),
-    (1, 1, 0), (0, 1, 1), (1, 1, 1), (0, 3, 1), (1, 1, 3), (0, 0, 3), (1, 3, 0), "inputs", 0, 1, (0, 2, 1), (1, 1, 2),
-    (0, 1, 3), (1, 3, 1), (0, 3, 3), (1, 3, 3), 2, 3, (0, 2, 3), (1, 3, 2), (0, 0, 2), (1, 2, 0), 4, (0, 1, 2),
-    (1, 2, 1), (0, 3, 2), (1, 2, 3), 5, 6, (0, 2, 2), (1, 2, 2), 7,
+    (1, 1, 0), (0, 1, 1), (1, 1, 1), (0, 3, 1), (1, 1, 3), (0, 0, 3), (1, 3, 0), "inputs", 0, 1, (0, 1, 3), (1, 3, 1),
+    (0, 3, 3), (1, 3, 3), 2, 3, (0, 2, 1), (1, 1, 2), (0, 0, 2), (1, 2, 0), 4, (0, 2, 3), (1, 3, 2), (0, 1, 2),
+    (0, 3, 2), 6, (1, 2, 1), (1, 2, 3), 5, (0, 2, 2), (1, 2, 2), 7,
 ]
 
 
@@ -56,7 +56,7 @@
 def kernel(
     li, og, ids, sb, kr, kc, out,
     kr_v, kc_v, gbuf, zb, z2, xq, xtb, xto, sg, stl, sts, sgs, idall, hm, mcol, lane_v, base_v, sgn_v, base_a, base_b,
-    sa0, sa1, sa2, sa3, sa4, sa5, sa6, sa7, ps, pd, r1, q2, r2,
+    sa0, sa1, sa2, sa3, ps, pd, r1, q2, r2,
     lo_, gs, gr, ss, sr, xs_, xr, xl, ds_, dr, ls, lt, sgss, sgr, km, s1, w1, s2, w2,
 ):
     d = lax.axis_index("doc")
@@ -326,7 +326,7 @@
 
     lax.fori_loop(0, 32, fly, 0)
 
-    stage = (sa0, sa1, sa2, sa3, sa4, sa5, sa6, sa7)
+    stage = (sa0, sa1, sa2, sa3)
     lanes = lax.broadcasted_iota(I32, (8, 128), 1)
     sub = lax.broadcasted_iota(I32, (128, 128), 0)
 
@@ -334,68 +334,72 @@
         for j in range(128):
             t[pl.ds(4 * j, 4), :] = z2[pl.ds(base[n, j], 4), :]
 
-    def settle(t, i, n):
-        h = jnp.where(parity(sub & lane_v[i, n:n + 1, :]) == 1, -1.0, 1.0).astype(BF16)
-        hi, lo = halves(t[...])
+    def settle(ta, tb, i, n):
+        h = jnp.concatenate(
+            [jnp.where(parity(sub & lane_v[i, n + b:n + b + 1, :]) == 1, -1.0, 1.0).astype(BF16) for b in range(2)],
+            axis=1,
+        )
+        both = [jnp.concatenate(halves(t[...]), axis=1) for t in (ta, tb)]
         r = jnp.dot(
-            jnp.concatenate([hi, lo], axis=1), jnp.concatenate([h, h], axis=0), preferred_element_type=F32
+            jnp.concatenate(both, axis=0), jnp.concatenate([h, h], axis=0), preferred_element_type=F32
         )
-        acc = [jnp.zeros((8, 128), F32) for _ in range(4)]
-        for q in range(64):
-            acc[q % 4] = jnp.where((lanes >> 1) == q, r[8 * q:8 * q + 8, :], acc[q % 4])
-        t = (acc[0] + acc[1]) + (acc[2] + acc[3])
-        t = jnp.where((lanes[:4] & 1) == 0, t[:4], t[4:])
-        for s in range(4):
-            ps[s, i, n:n + 1, :] = t[s:s + 1, :]
-
-    def round_(new, index, base, m, old):
-        index(m).wait()
-        for n in range(4):
-            fetch(new[n], base, n)
-            if old is not None:
-                settle(old[n], m - 1, n)
-        index(jnp.minimum(m + 2, 15)).start()
+        for b in range(2):
+            acc = [jnp.zeros((8, 128), F32) for _ in range(4)]
+            for q in range(64):
+                o = 512 * b + 8 * q
+                acc[q % 4] = jnp.where((lanes >> 1) == q, r[o:o + 8, 128 * b:128 * b + 128], acc[q % 4])
+            t = (acc[0] + acc[1]) + (acc[2] + acc[3])
+            t = jnp.where((lanes[:4] & 1) == 0, t[:4], t[4:])
+            for s in range(4):
+                ps[s, i, n + b:n + b + 1, :] = t[s:s + 1, :]
 
     def pick(i, carry):
-        round_(stage[4:], index_b, base_b, 2 * i + 1, stage[:4])
-        round_(stage[:4], index_a, base_a, 2 * i + 2, stage[4:])
+        for k, (index, base) in enumerate(((index_a, base_a), (index_b, base_b))):
+            m = 2 * i + k
+            index(m).wait()
+            for n in range(4):
+                fetch(stage[n], base, n)
+            index(jnp.minimum(m + 2, 15)).start()
+            settle(stage[0], stage[1], m, 0)
+            settle(stage[2], stage[3], m, 2)
         return carry
 
-    round_(stage[:4], index_a, base_a, 0, None)
-    lax.fori_loop(0, 7, pick, 0)
-    index_b(15).wait()
-    for n in range(4):
-        fetch(stage[4 + n], base_b, n)
-        settle(stage[n], 14, n)
-    for n in range(4):
-        settle(stage[4 + n], 15, n)
+    me8 = d * 2 + zh
+
+    def emit(part):
+        at = 8 * part
+        big = jnp.broadcast_to(idall[2, 0:1, 0:1], (8, 4, 128))
+        sign = sgn_v[at:at + 8]
+        for e in range(4):
+            t = jnp.where(big > e, ps[min(e + 1, 3), at:at + 8], ps[e, at:at + 8])
+            t = jnp.where(big == e, ps[0, at:at + 8], t) * sign
+            for h in range(2):
+                for i in range(2):
+                    pd[part, e * 2 + h, i, 0:4] = t[i * 4 + h * 2]
+                    pd[part, e * 2 + h, i, 4:8] = t[i * 4 + h * 2 + 1]
+        r1[part, me8] = pd[part, me8]
+        for n, (k, m) in enumerate(line):
+            tz, tc = (z + k) % 4, (c + m) % 2
+            dest = ((tz % 2) * 2 + tc) * 2 + tz // 2
+            cp = remote(pd.at[part, dest], r1.at[part, me8], s1.at[part, n], w1.at[part, me8], mate(k, m))
+            cp.start()
+            pending.append(cp)
+
+    lax.fori_loop(0, 4, pick, 0)
+    emit(0)
+    lax.fori_loop(4, 8, pick, 0)
+    emit(1)
     index_a(0).wait()
-
-    big = jnp.broadcast_to(idall[2, 0:1, 0:1], (16, 4, 128))
-    sign = sgn_v[...]
-    for e in range(4):
-        t = jnp.where(big > e, ps[min(e + 1, 3)], ps[e])
-        t = jnp.where(big == e, ps[0], t) * sign
-        for h in range(2):
-            for i in range(4):
-                pd[e * 2 + h, i, 0:4] = t[i * 4 + h * 2]
-                pd[e * 2 + h, i, 4:8] = t[i * 4 + h * 2 + 1]
-    me8 = d * 2 + zh
-    r1[me8] = pd[me8]
-    for n, (k, m) in enumerate(line):
-        tz, tc = (z + k) % 4, (c + m) % 2
-        dest = ((tz % 2) * 2 + tc) * 2 + tz // 2
-        cp = remote(pd.at[dest], r1.at[me8], s1.at[n], w1.at[me8], mate(k, m))
-        cp.start()
-        pending.append(cp)
-    for k, m in line:
-        tz, tc = (z + k) % 4, (c + m) % 2
-        src = ((tz % 2) * 2 + tc) * 2 + tz // 2
-        remote(pd.at[src], r1.at[src], s1.at[0], w1.at[src], sibling).wait_recv()
+    index_b(0).wait()
+    for part in range(2):
+        for k, m in line:
+            tz, tc = (z + k) % 4, (c + m) % 2
+            src = ((tz % 2) * 2 + tc) * 2 + tz // 2
+            remote(pd.at[part, src], r1.at[part, src], s1.at[part, 0], w1.at[part, src], sibling).wait_recv()
     for i in range(4):
-        t = r1[0, i]
+        t = r1[i // 2, 0, i % 2]
         for n in range(1, 8):
-            t = t + r1[n, i]
+            t = t + r1[i // 2, n, i % 2]
         for j in range(4):
             q2[i * 4 + j, 0:2, :] = t[2 * j:2 * j + 2, :]
             q2[i * 4 + j, 2:8, :] = jnp.zeros((6, 128), F32)
@@ -453,19 +457,15 @@
         pltpu.VMEM((512, 128), F32),
         pltpu.VMEM((512, 128), F32),
         pltpu.VMEM((512, 128), F32),
-        pltpu.VMEM((512, 128), F32),
-        pltpu.VMEM((512, 128), F32),
-        pltpu.VMEM((512, 128), F32),
-        pltpu.VMEM((512, 128), F32),
         pltpu.VMEM((4, 16, 4, 128), F32),
-        pltpu.VMEM((8, 4, 8, 128), F32),
-        pltpu.VMEM((8, 4, 8, 128), F32),
+        pltpu.VMEM((2, 8, 2, 8, 128), F32),
+        pltpu.VMEM((2, 8, 2, 8, 128), F32),
         pltpu.VMEM((16, 8, 128), F32),
         pltpu.VMEM((16, 8, 128), F32),
         dma((4,)), dma((31,)), dma((2, 4, 4)), dma((2, 4, 4)), dma((2, 4, 4)),
         dma((5,)), dma((4,)), dma(()), dma((3,)), dma((4,)),
         dma((8,)), dma((16,)), dma((8,)), dma((8, 2)), dma((2,)),
-        dma((7,)), dma((8,)), dma((15,)), dma((16,)),
+        dma((2, 7)), dma((2, 8)), dma((15,)), dma((16,)),
     ]
     got = pl.pallas_call(
         kernel,

time: 66.6 us -> 65.8 us (0.988)
  Pallas kernels: 65.2 us -> 64.3 us
    pallas_call x1, Pallas kernels: 65.2 us -> 64.3 us  [on_device(): pl.pallas_call(kernel, out_shape=jax.ShapeDtypeStruct((8, 128), F32), in_...]
where the time goes in v4:
time: 65.8 us; the launch traced here: 65.5 us
  Pallas kernels  64.3 us (98%)
  local copies, waits for them, and re-layouts  1.25 us (2%)
    pallas_call x1, Pallas kernels, on_device(): pl.pallas_call(kernel, out_shape=jax.ShapeDtypeStruct((8, 128), F32), in_...  64.3 us

profile of v4, /device:TPU:0, one launch (start us, length us, event | category | flops | bytes accessed | tf_op | source)
XLA Modules:
  0.0 65.5 jit_solution(3864486642480333618)
XLA Ops:
  0.0 64.3 %sketch.1 = f32[8,128]{1,0:T(8,128)} custom-call(bf16[512,256]{1,0:T(8,128)(2,1)} %li.1, bf16[512,256]{1,0:T(8,128)(2,1)} %og.1, s32[4,128]{1,0:T(4,128)} %bitcast.6, s32[256,8192]{1,0:T(8,128)} %sb.1, s32[16,4,128]{2,1,0:T(4,128)} %bitcast.4, s32[16,4,128]{2,1,0:T(4,128)} %bitcast.5), custom_call_target="tpu_custom_call" | custom-call | tf_op jit(solution)/shard_map/sketch/pallas_call | solution.py:470
  64.3 1.2 %slice.3 = f32[2,128]{1,0:T(2,128)} slice(f32[8,128]{1,0:T(8,128)} %sketch.1), slice={[0:2], [0:128]} | slice | bytes 2048 | tf_op jit(solution)/shard_map/slice | solution.py:484

commit v5 on v4

--- a/solution.py
+++ b/solution.py
@@ -16,9 +16,9 @@
 ]
 OPS = [
     (1, 0, 0), (0, 1, 0), (0, 3, 0), "relay", (1, 0, 1), (1, 0, 3), "signs", (0, 2, 0), (1, 0, 2), (0, 0, 1),
-    (1, 1, 0), (0, 1, 1), (1, 1, 1), (0, 3, 1), (1, 1, 3), (0, 0, 3), (1, 3, 0), "inputs", 0, 1, (0, 1, 3), (1, 3, 1),
-    (0, 3, 3), (1, 3, 3), 2, 3, (0, 2, 1), (1, 1, 2), (0, 0, 2), (1, 2, 0), 4, (0, 2, 3), (1, 3, 2), (0, 1, 2),
-    (0, 3, 2), 6, (1, 2, 1), (1, 2, 3), 5, (0, 2, 2), (1, 2, 2), 7,
+    (1, 1, 0), (0, 1, 1), (1, 1, 1), (0, 3, 1), (1, 1, 3), (0, 0, 3), (1, 3, 0), (0, 1, 3), (1, 3, 1), (0, 3, 3),
+    (1, 3, 3), "inputs", 0, (0, 2, 1), (1, 1, 2), 1, (0, 0, 2), (1, 2, 0), 2, (0, 2, 3), (1, 3, 2), 3, (0, 1, 2),
+    (0, 3, 2), 4, (1, 2, 1), (1, 2, 3), 6, (0, 2, 2), (1, 2, 2), 5, 7,
 ]
 
 

time: 65.8 us -> 59.5 us (0.904)
  Pallas kernels: 64.3 us -> 57.9 us
    pallas_call x1, Pallas kernels: 64.3 us -> 57.9 us  [on_device(): pl.pallas_call(kernel, out_shape=jax.ShapeDtypeStruct((8, 128), F32), in_...]
where the time goes in v5:
time: 59.5 us; the launch traced here: 59.2 us
  Pallas kernels  57.9 us (97%)
  local copies, waits for them, and re-layouts  1.25 us (2%)
    pallas_call x1, Pallas kernels, on_device(): pl.pallas_call(kernel, out_shape=jax.ShapeDtypeStruct((8, 128), F32), in_...  57.9 us
    slice x1, local copies, waits for them, and re-layouts, on_device(): return got[:2].reshape(1, 256)  1.25 us

profile of v5, /device:TPU:0, one launch (start us, length us, event | category | flops | bytes accessed | tf_op | source)
XLA Modules:
  0.0 59.2 jit_solution(4634302387968947721)
XLA Ops:
  0.0 57.9 %sketch.1 = f32[8,128]{1,0:T(8,128)} custom-call(bf16[512,256]{1,0:T(8,128)(2,1)} %li.1, bf16[512,256]{1,0:T(8,128)(2,1)} %og.1, s32[4,128]{1,0:T(4,128)} %bitcast.6, s32[256,8192]{1,0:T(8,128)} %sb.1, s32[16,4,128]{2,1,0:T(4,128)} %bitcast.4, s32[16,4,128]{2,1,0:T(4,128)} %bitcast.5), custom_call_target="tpu_custom_call" | custom-call | tf_op jit(solution)/shard_map/sketch/pallas_call | solution.py:470
  58.0 1.2 %slice.3 = f32[2,128]{1,0:T(2,128)} slice(f32[8,128]{1,0:T(8,128)} %sketch.1), slice={[0:2], [0:128]} | slice | bytes 2048 | tf_op jit(solution)/shard_map/slice | solution.py:484

commit v6 on v5

--- a/solution.py
+++ b/solution.py
@@ -115,11 +115,6 @@
     for a in range(16):
         keeps.append(pltpu.make_async_copy(sb.at[:, pl.ds(column(a, zh, zl), 128)], stl.at[a], lt.at[a]))
 
-    @pl.when(c == zh)
-    def _():
-        for cp in keeps:
-            cp.start()
-
     pl.semaphore_wait(bar, len(ring) + len(line))
 
     def remote(src, dst, s, r, to):
@@ -179,6 +174,11 @@
     @pl.when(c == zh)
     def _():
         own_x.start()
+
+    @pl.when(c == zh)
+    def _():
+        for cp in keeps:
+            cp.start()
 
     relays = []
     for k in range(2):

time: 59.5 us -> 59.5 us (level)
  no operation moved by 1% of the time
where the time goes in v6:
time: 59.5 us; the launch traced here: 59.2 us
  Pallas kernels  58 us (97%)
  local copies, waits for them, and re-layouts  1.25 us (2%)
    pallas_call x1, Pallas kernels, on_device(): pl.pallas_call(kernel, out_shape=jax.ShapeDtypeStruct((8, 128), F32), in_...  58 us
    slice x1, local copies, waits for them, and re-layouts, on_device(): return got[:2].reshape(1, 256)  1.25 us

profile of v6, /device:TPU:0, one launch (start us, length us, event | category | flops | bytes accessed | tf_op | source)
XLA Modules:
  0.0 59.2 jit_solution(15373961314375149341)
XLA Ops:
  0.0 58.0 %sketch.1 = f32[8,128]{1,0:T(8,128)} custom-call(bf16[512,256]{1,0:T(8,128)(2,1)} %li.1, bf16[512,256]{1,0:T(8,128)(2,1)} %og.1, s32[4,128]{1,0:T(4,128)} %bitcast.6, s32[256,8192]{1,0:T(8,128)} %sb.1, s32[16,4,128]{2,1,0:T(4,128)} %bitcast.4, s32[16,4,128]{2,1,0:T(4,128)} %bitcast.5), custom_call_target="tpu_custom_call" | custom-call | tf_op jit(solution)/shard_map/sketch/pallas_call | solution.py:470
  58.0 1.2 %slice.3 = f32[2,128]{1,0:T(2,128)} slice(f32[8,128]{1,0:T(8,128)} %sketch.1), slice={[0:2], [0:128]} | slice | bytes 2048 | tf_op jit(solution)/shard_map/slice | solution.py:484
